TPU v7x, 32 devices: a whole 2x2x4 slice. The times are simulated.
32 devices in a mesh: groups: 2 (over y), row: 4 (over x, core), col: 4 (over z).
Axes of the slice: x: 2, y: 2, z: 4, core: 2. Of those that a mesh axis runs over, the one named last changes fastest.
Arguments:
- adjacency: bfloat16 [8, 4, 32, 128, 128], P(('groups', 'row'), 'col'), parts along dimension 0, may hold values from 0.049804688 to 1
- tile_row: int32 [8, 4, 32], P(('groups', 'row'), 'col'), parts along dimension 0, may hold values from -1 to 7, as said below
- tile_col: int32 [8, 4, 32], P(('groups', 'row'), 'col'), parts along dimension 0, may hold values from -1 to 7, as said below
- seed_node: int32 [512], P('groups'), parts along dimension 0, may hold values from 0 to 4095
- teleport_block: int32 [512], P('groups'), parts along dimension 0, may hold values from 0 to 31
- previous: float32 [8192, 256], P(('groups', 'row', 'col')), parts along dimension 0, may hold values from 0.1 to 10
Outputs:
- rank_field: float32 [8192, 256], P(('groups', 'row', 'col')), parts along dimension 0
There are 2 independent parts, one for each index of `groups`. A program takes and returns all parts, laid end to end along the dimension named above; each array names one. Nothing has to cross between parts.
Inputs may be any that keep to these rules, and one draw needn't show every extreme that they name: On each device the slots with entries >= 0 come first, and tile_row and tile_col are -1 together on the other slots; a device's (tile_row, tile_col) pairs are distinct; in every part exactly one device has all 32 slots used and every other device uses between 5 and 10 of them. `tile_col`: empty exactly where tile_row is empty. In every part, for each index of row, at least one tile column holds no tile on any device with that index of row.
All inputs are finite; a program needn't handle non-finite values.
Results may differ from a plain program's by a relative error of at most 0.0003.
Values may be sent and summed in bfloat16 or wider, within the bound.
A program may use at most 64 MiB of HBM per device.

v0:
```python
import jax
import jax.numpy as jnp
from jax import lax
from jax.sharding import PartitionSpec as P

TILE = 128
ITERS = 3
damping = 0.85
highest = lax.Precision.HIGHEST


def teleport_weights(node_ids, seed_node, teleport_block):
    at_seed = (node_ids[:, None] == seed_node[None, :]).astype(jnp.float32)
    in_block = ((node_ids // TILE)[:, None] == teleport_block[None, :]).astype(jnp.float32)
    return 4.0 * at_seed + 2.0 * in_block


def block_sum(
    tile_stack, row_ids, col_ids, ordering, sorted_keys, rank_panel, first_row, block_rows
):
    slot_total = tile_stack.shape[0]
    tile_edge = tile_stack.shape[1]
    seed_width = rank_panel.shape[2]
    slot_batch = min(8, slot_total)
    first_live = jnp.sum((sorted_keys < first_row).astype(jnp.int32))
    past_live = jnp.sum((sorted_keys < first_row + block_rows).astype(jnp.int32))
    batches = (past_live - first_live + slot_batch - 1) // slot_batch

    def one_batch(batch_index, accumulated):
        for offset in range(slot_batch):
            position = first_live + batch_index * slot_batch + offset
            slot_index = lax.dynamic_index_in_dim(
                ordering, jnp.minimum(position, slot_total - 1), 0, keepdims=False
            )
            is_live = position < past_live
            target_row = lax.dynamic_index_in_dim(row_ids, slot_index, 0, keepdims=False)
            source_col = lax.dynamic_index_in_dim(col_ids, slot_index, 0, keepdims=False)
            target = jnp.clip(target_row - first_row, 0, block_rows - 1)
            source = jnp.maximum(source_col, 0)
            one_tile = lax.dynamic_index_in_dim(tile_stack, slot_index, 0, keepdims=False)
            panel_block = lax.dynamic_index_in_dim(rank_panel, source, 0, keepdims=False)
            product = jnp.dot(one_tile, panel_block, preferred_element_type=jnp.float32)
            current = lax.dynamic_index_in_dim(accumulated, target, 0, keepdims=False)
            updated = current + jnp.where(is_live, product, jnp.zeros_like(product))
            accumulated = lax.dynamic_update_index_in_dim(accumulated, updated, target, 0)
        return accumulated

    start_sum = jnp.zeros((block_rows, tile_edge, seed_width), jnp.float32)
    result = lax.fori_loop(0, batches, one_batch, start_sum)
    return result.reshape(block_rows * tile_edge, seed_width)


def on_device(adjacency, tile_row, tile_col, seed_node, teleport_block, previous):
    tile_stack = adjacency[0, 0]
    row_ids = tile_row[0, 0]
    col_ids = tile_col[0, 0]
    owned_rows, seed_width = previous.shape
    slot_total = tile_stack.shape[0]
    tile_edge = tile_stack.shape[1]
    row_devices = lax.axis_size("row")
    col_devices = lax.axis_size("col")
    tile_rows = owned_rows * row_devices // tile_edge
    tile_cols = owned_rows * col_devices // tile_edge
    sort_keys = jnp.where(row_ids >= 0, row_ids, tile_rows)
    slot_order = jnp.arange(slot_total, dtype=jnp.int32)
    sorted_keys, ordering = lax.sort((sort_keys, slot_order), num_keys=1, is_stable=True)
    col_place = (col_ids[:, None] == jnp.arange(tile_cols, dtype=jnp.int32)[None, :]).astype(
        jnp.float32
    )
    tile_sums = jnp.sum(tile_stack.astype(jnp.float32), axis=1)
    col_sums = jnp.einsum("tj,tb->jb", col_place, tile_sums, precision=highest).reshape(
        tile_cols * tile_edge
    )
    full_divisor = jnp.maximum(lax.psum(col_sums, "col"), 1.0)
    first_node = (lax.axis_index("row") * col_devices + lax.axis_index("col")) * owned_rows
    node_ids = first_node + jnp.arange(owned_rows, dtype=jnp.int32)
    teleport = teleport_weights(node_ids, seed_node, teleport_block)
    rank_field = previous
    for iteration in range(ITERS):
        gathered = lax.all_gather(rank_field, "col", axis=0, tiled=True)
        rank_panel = (gathered / full_divisor[:, None]).astype(jnp.bfloat16)
        rank_panel = rank_panel.reshape(tile_cols, tile_edge, seed_width)
        partial_sum = block_sum(
            tile_stack, row_ids, col_ids, ordering, sorted_keys, rank_panel, 0, tile_rows
        )
        summed = lax.psum_scatter(partial_sum, "row", scatter_dimension=0, tiled=True)
        rank_field = damping * summed + (1.0 - damping) * teleport
    return rank_field


def solution(mesh):
    in_specs = (
        P(("groups", "row"), "col", None, None, None),
        P(("groups", "row"), "col", None),
        P(("groups", "row"), "col", None),
        P("groups"),
        P("groups"),
        P(("groups", "row", "col"), None),
    )
    out_specs = P(("groups", "row", "col"), None)
    return jax.shard_map(
        on_device, mesh=mesh, in_specs=in_specs, out_specs=out_specs, check_vma=False
    )
```

profile of v0, /device:TPU:0, one launch (start us, length us, event | category | flops | bytes accessed | tf_op | source)
XLA Modules:
  0.0 590.8 jit_solution(7642503846385073427)
XLA Ops:
  6.5 0.7 all-gather.4.cloned.1.call-update
  7.3 0.0 reduce-scatter.4.cloned.1.call-start
  7.3 0.7 compare_select_fusion
  8.0 1.1 sort.15
  9.0 0.7 fusion.195
  11.1 1.4 convert_reduce_fusion
  12.5 0.3 convolution_bitcast_fusion
  12.7 13.6 %psum.7 = f32[1024]{0:T(1024)S(1)} all-reduce(f32[1024]{0:T(1024)S(1)} %convolution_bitcast_fusion), channel_id=1, replica_groups=mesh['groups'=2,'row'=4,'col'=4] {'col'}, use_global_device_ids=true, to_apply=%region_4.5 | all-reduce | flops 1024 | bytes 8192 | tf_op jit(solution)/shard_map/psum | solution.py:74
  26.4 13.3 %all-gather.4.cloned.1.call-done = f32[1024,256]{1,0:T(8,128)} async-done(((f32[256,256]{1,0:T(8,128)}), f32[1024,256]{1,0:T(8,128)}) %all-gather.4.cloned.1.call-update) | async-done | bytes 1048592 | tf_op jit(solution)/shard_map/all_gather | solution.py:80
  39.6 1.4 divide_convert_fusion.2
  41.1 0.1 broadcast.71.clone.1
  41.2 33.7 %while.30 = (s32[]{:T(128)}, f32[8,128,256]{2,1,0:T(8,128)S(1)}, s32[]{:T(128)}, s32[]{:T(128)}, s32[32]{0:T(128)S(1)}, /*index=5*/s32[32]{0:T(128)S(1)}, s32[]{...) while((s32[]{:T(128)}, f32[8,128,256]{2,1,0:T(8,128)S(1)}, ...), condition=%wide.region_6.7_spmd, body=%wide.region_5.6_spmd.sunk | while | flops 67633232 | bytes 4982441 | solution.py:49
  41.9 0.7 fusion.300
  57.6 0.7 fusion.301
  60.3 0.2 fusion.302
  62.3 0.2 fusion.303
  64.5 0.2 fusion.304
  66.5 0.2 fusion.305
  68.5 0.2 fusion.306
  70.5 0.2 fusion.307
  72.6 0.2 fusion.308
  74.7 0.2 fusion.309
  74.9 0.9 copy-done.1
  75.9 0.0 reduce-scatter.4.cloned.1.call-update
  75.9 0.0 all-gather.6.cloned.1.call-start
  76.0 124.4 %reduce-scatter.4.cloned.1.call-done = f32[256,256]{1,0:T(8,128)} async-done(((f32[1024,256]{1,0:T(8,128)}), f32[256,256]{1,0:T(8,128)}) %reduce-scatter.4.cloned.1.call-update) | async-done | bytes 262160 | tf_op jit(solution)/shard_map/reduce_scatter | solution.py:86
  200.4 1.8 fusion.192
  202.2 0.0 reduce-scatter.6.cloned.1.call-start
  202.2 28.1 %all-gather.6.cloned.1.call-done = f32[1024,256]{1,0:T(8,128)} async-done(((f32[256,256]{1,0:T(8,128)}), f32[1024,256]{1,0:T(8,128)}) %all-gather.6.cloned.1.call-update) | async-done | bytes 1048592 | tf_op jit(solution)/shard_map/all_gather | solution.py:80
  230.3 1.4 divide_convert_fusion.1
  231.7 0.1 broadcast.71.clone
  231.8 33.8 %while.31 = (s32[]{:T(128)}, f32[8,128,256]{2,1,0:T(8,128)S(1)}, s32[]{:T(128)}, s32[]{:T(128)}, s32[32]{0:T(128)S(1)}, /*index=5*/s32[32]{0:T(128)S(1)}, s32[]{...) while((s32[]{:T(128)}, f32[8,128,256]{2,1,0:T(8,128)S(1)}, ...), condition=%wide.region_9.10_spmd, body=%wide.region_8.9_spmd.sunk | while | flops 67633232 | bytes 4982441 | solution.py:49
  232.5 0.7 fusion.326
  248.3 0.7 fusion.327
  251.0 0.2 fusion.328
  253.1 0.2 fusion.329
  255.1 0.2 fusion.330
  257.2 0.2 fusion.331
  259.2 0.2 fusion.332
  261.2 0.2 fusion.333
  263.3 0.2 fusion.334
  265.5 0.2 fusion.335
  265.7 1.0 copy-done.2
  266.6 0.0 all-gather.8.cloned.1.call-start
  266.7 124.6 %reduce-scatter.6.cloned.1.call-done = f32[256,256]{1,0:T(8,128)} async-done(((f32[1024,256]{1,0:T(8,128)}), f32[256,256]{1,0:T(8,128)}) %reduce-scatter.6.cloned.1.call-update) | async-done | bytes 262160 | tf_op jit(solution)/shard_map/reduce_scatter | solution.py:86
  391.3 1.8 multiply_add_fusion.1
  393.1 0.0 reduce-scatter.8.cloned.1.call-start
  393.2 28.0 %all-gather.8.cloned.1.call-done = f32[1024,256]{1,0:T(8,128)} async-done(((f32[256,256]{1,0:T(8,128)}), f32[1024,256]{1,0:T(8,128)}) %all-gather.8.cloned.1.call-update) | async-done | bytes 1048592 | tf_op jit(solution)/shard_map/all_gather | solution.py:80
  421.2 1.4 divide_convert_fusion
  422.6 0.1 broadcast.71
  422.7 33.8 %while.32 = (s32[]{:T(128)}, f32[8,128,256]{2,1,0:T(8,128)S(1)}, s32[]{:T(128)}, s32[]{:T(128)}, s32[32]{0:T(128)S(1)}, /*index=5*/s32[32]{0:T(128)S(1)}, s32[]{...) while((s32[]{:T(128)}, f32[8,128,256]{2,1,0:T(8,128)S(1)}, ...), condition=%wide.region_12.13_spmd, body=%wide.region_11.12_spmd.sunk | while | flops 67633232 | bytes 4982441 | solution.py:49
  423.5 0.7 fusion.352
  439.2 0.7 fusion.353
  441.9 0.2 fusion.354
  444.0 0.2 fusion.355
  446.0 0.2 fusion.356
  448.1 0.2 fusion.357
  450.1 0.2 fusion.358
  452.2 0.2 fusion.359
  454.2 0.2 fusion.360
  456.4 0.2 fusion.361
  456.6 1.0 copy-done
  457.5 124.6 %reduce-scatter.8.cloned.1.call-done = f32[256,256]{1,0:T(8,128)} async-done(((f32[1024,256]{1,0:T(8,128)}), f32[256,256]{1,0:T(8,128)}) %reduce-scatter.8.cloned.1.call-update) | async-done | bytes 262160 | tf_op jit(solution)/shard_map/reduce_scatter | solution.py:86
  582.2 1.8 multiply_add_fusion
  (45 shorter events, 0.5 us)
Async XLA Ops:
  6.5 5.9 %copy-start.5 = (s32[1,1,32]{2,1,0:T(1,128)S(1)}, s32[1,1,32]{2,1,0:T(1,128)}, u32[]{:S(2)}) copy-start(s32[1,1,32]{2,1,0:T(1,128)} %param.14) | copy-start | bytes 388
  6.5 33.1 %all-gather.4.cloned.1.call-start = ((), (), s32[]{:S(2)}) async-start(), calls=%async_computation.3 | async-start | bytes 1310720 | tf_op jit(solution)/shard_map/all_gather | solution.py:80
  7.3 193.1 %reduce-scatter.4.cloned.1.call-start = ((), (), s32[]{:S(2)}) async-start(), calls=%async_computation.4 | async-start | bytes 1310720 | tf_op jit(solution)/shard_map/reduce_scatter | solution.py:86
  26.4 14.8 %copy-start.3 = (bf16[1,1,32,128,128]{4,3,2,1,0:T(8,128)(2,1)S(1)}, bf16[1,1,32,128,128]{4,3,2,1,0:T(8,128)(2,1)}, u32[]{:S(2)}) copy-start(bf16[1,1,32,128,128]{4,3,2,1,0:T(8,128)(2,1)} %param.12) | copy-start | bytes 3145732
  26.4 14.8 %copy-start.4 = (s32[1,1,32]{2,1,0:T(1,128)S(1)}, s32[1,1,32]{2,1,0:T(1,128)}, u32[]{:S(2)}) copy-start(s32[1,1,32]{2,1,0:T(1,128)} %param.13) | copy-start | bytes 388
  74.9 1.0 copy-start.1
  74.9 125.5 %copy-start.6 = (s32[256]{0:T(256)S(1)}, s32[256]{0:T(256)}, u32[]{:S(2)}) copy-start(s32[256]{0:T(256)} %param.16) | copy-start | bytes 3076
  74.9 125.4 %copy-start.7 = (s32[256]{0:T(256)S(1)}, s32[256]{0:T(256)}, u32[]{:S(2)}) copy-start(s32[256]{0:T(256)} %param.15) | copy-start | bytes 3076
  75.9 154.4 %all-gather.6.cloned.1.call-start = ((), (), s32[]{:S(2)}) async-start(), calls=%async_computation.5 | async-start | bytes 1310720 | tf_op jit(solution)/shard_map/all_gather | solution.py:80
  202.2 189.1 %reduce-scatter.6.cloned.1.call-start = ((), (), s32[]{:S(2)}) async-start(), calls=%async_computation.6 | async-start | bytes 1310720 | tf_op jit(solution)/shard_map/reduce_scatter | solution.py:86
  265.6 1.0 copy-start.2
  266.6 154.6 %all-gather.8.cloned.1.call-start = ((), (), s32[]{:S(2)}) async-start(), calls=%async_computation.7 | async-start | bytes 1310720 | tf_op jit(solution)/shard_map/all_gather | solution.py:80
  393.1 189.1 %reduce-scatter.8.cloned.1.call-start = ((), (), s32[]{:S(2)}) async-start(), calls=%async_computation.8 | async-start | bytes 1310720 | tf_op jit(solution)/shard_map/reduce_scatter | solution.py:86
  456.5 1.0 copy-start
Sparse Core Ops, SparseCore 0:
  8.9 30.6 all-gather.3
  76.0 124.3 reduce-scatter.3
  202.3 27.9 all-gather.5
  266.8 124.4 reduce-scatter.5
  393.2 27.9 all-gather.7
  457.7 124.4 reduce-scatter.7
where the time goes:
time: 596 us; the launch traced here: 591 us
  waiting for transfers between devices  444 us (74%)
  loops' own time  92.9 us (16%)
  between operations  14.9 us (2%)
  other arithmetic  13.6 us (2%)
  blocking collectives  13.6 us (2%)
  local copies, waits for them, and re-layouts  7.78 us (1%)
    reduce_scatter x3, waiting for transfers between devices, on_device(): lax.psum_scatter(partial_sum, 'row', scatter_dimension=0, tiled=True)  374 us
    another operation x3, loops' own time, block_sum(): result = lax.fori_loop(0, batches, one_batch, start_sum)  92.9 us
    all_gather x3, waiting for transfers between devices, on_device(): gathered = lax.all_gather(rank_field, 'col', axis=0, tiled=True)  69.4 us
    psum x1, blocking collectives, on_device(): full_divisor = jnp.maximum(lax.psum(col_sums, 'col'), 1.0)  13.6 us
  transfers between devices with their start and end apart: 6, of which 6 were waited for; matrix products, arithmetic and copies ran while one was open for 1% of the time, Pallas kernels for 0%

commit v1 on v0

--- a/solution.py
+++ b/solution.py
@@ -77,7 +77,25 @@
     teleport = teleport_weights(node_ids, seed_node, teleport_block)
     rank_field = previous
     for iteration in range(ITERS):
-        gathered = lax.all_gather(rank_field, "col", axis=0, tiled=True)
+        peers, index, rows = (lax.axis_size("col"), lax.axis_index("col"), rank_field.shape[0])
+        right = [(i, (i + 1) % peers) for i in range(peers)]
+        behind = [(i, (i - 1) % peers) for i in range(peers)]
+        gathered = jnp.zeros(
+            (*rank_field.shape[:0], peers * rows, *rank_field.shape[0 + 1 :]), rank_field.dtype
+        )
+        gathered = lax.dynamic_update_slice_in_dim(gathered, rank_field, index * rows, axis=0)
+        from_left = from_right = rank_field
+        middle = peers // 2
+        for step in range(1, middle + 1):
+            from_left = lax.ppermute(from_left, "col", right)
+            gathered = lax.dynamic_update_slice_in_dim(
+                gathered, from_left, (index - step) % peers * rows, axis=0
+            )
+            if step < peers - middle:
+                from_right = lax.ppermute(from_right, "col", behind)
+                gathered = lax.dynamic_update_slice_in_dim(
+                    gathered, from_right, (index + step) % peers * rows, axis=0
+                )
         rank_panel = (gathered / full_divisor[:, None]).astype(jnp.bfloat16)
         rank_panel = rank_panel.reshape(tile_cols, tile_edge, seed_width)
         partial_sum = block_sum(

time: 596 us -> 559 us (0.938)
  waiting for transfers between devices: 444 us -> 401 us
  starting transfers between devices: 0.21 us -> 13.3 us
  other arithmetic: 13.6 us -> 5.86 us
    all_gather x3 -> x0, waiting for transfers between devices: 69.4 us -> none  [on_device(): gathered = lax.all_gather(rank_field, 'col', axis=0, tiled=True)]
    ppermute x0 -> x9, waiting for transfers between devices: none -> 40.5 us  [the longest x6 31.9 us: on_device(): from_left = lax.ppermute(from_left, 'col', right)]
    ppermute x0 -> x9, starting transfers between devices: none -> 13.2 us  [the longest x3 6.73 us: on_device(): from_right = lax.ppermute(from_right, 'col', behind)]
    reduce_scatter x3, waiting for transfers between devices: 374 us -> 361 us  [on_device(): lax.psum_scatter(partial_sum, 'row', scatter_dimension=0, tiled=True)]
  transfers between devices with their start and end apart: 6 -> 12, of which waited for: 6 -> 10; matrix products, arithmetic and copies ran while one was open for 1% -> 1% of each run, Pallas kernels for 0% -> 0%
where the time goes in v1:
time: 559 us; the launch traced here: 554 us
  waiting for transfers between devices  401 us (72%)
  loops' own time  90.4 us (16%)
  between operations  14.6 us (3%)
  blocking collectives  13.9 us (2%)
  starting transfers between devices  13.3 us (2%)
  local copies, waits for them, and re-layouts  10.9 us (2%)
  other arithmetic  5.86 us (1%)
    reduce_scatter x3, waiting for transfers between devices, on_device(): lax.psum_scatter(partial_sum, 'row', scatter_dimension=0, tiled=True)  361 us
    another operation x3, loops' own time, block_sum(): result = lax.fori_loop(0, batches, one_batch, start_sum)  90.4 us
    ppermute x6, waiting for transfers between devices, on_device(): from_left = lax.ppermute(from_left, 'col', right)  31.9 us
    psum x1, blocking collectives, on_device(): full_divisor = jnp.maximum(lax.psum(col_sums, 'col'), 1.0)  13.9 us
  transfers between devices with their start and end apart: 12, of which 10 were waited for; matrix products, arithmetic and copies ran while one was open for 1% of the time, Pallas kernels for 0%

profile of v1, /device:TPU:0, one launch (start us, length us, event | category | flops | bytes accessed | tf_op | source)
XLA Modules:
  0.0 554.1 jit_solution(12755256588937974636)
XLA Ops:
  6.5 3.0 collective-permute-start
  9.6 2.1 collective-permute-start.1
  11.7 1.5 convert_reduce_fusion
  13.1 0.2 convolution_bitcast_fusion
  13.4 13.9 %psum.7 = f32[1024]{0:T(1024)S(1)} all-reduce(f32[1024]{0:T(1024)S(1)} %convolution_bitcast_fusion), channel_id=1, replica_groups=mesh['groups'=2,'row'=4,'col'=4] {'col'}, use_global_device_ids=true, to_apply=%region_4.5 | all-reduce | flops 1024 | bytes 8192 | tf_op jit(solution)/shard_map/psum | solution.py:74
  27.4 1.1 sort.15
  28.5 0.3 collective-permute-start.2
  28.8 0.6 fusion.195
  30.7 6.0 %collective-permute-done.2 = f32[256,256]{1,0:T(8,128)S(1)} collective-permute-done((f32[256,256]{1,0:T(8,128)S(1)}, f32[256,256]{1,0:T(8,128)S(1)}, u32[]{:S(2)}, u32[]{:S(2)}) %collective-permute-start.2) | collective-permute-done | bytes 262176 | tf_op jit(solution)/shard_map/ppermute | solution.py:90
  36.8 0.2 divide_convert_fusion.2
  37.1 0.9 copy-done.3
  38.0 33.0 %while.30 = (s32[]{:T(128)}, f32[8,128,256]{2,1,0:T(8,128)S(1)}, s32[]{:T(128)}, s32[]{:T(128)}, s32[32]{0:T(128)S(1)}, /*index=5*/s32[32]{0:T(128)S(1)}, s32[]{...) while((s32[]{:T(128)}, f32[8,128,256]{2,1,0:T(8,128)S(1)}, ...), condition=%wide.region_6.7_spmd, body=%wide.region_5.6_spmd.sunk | while | flops 67633232 | bytes 4982441 | solution.py:49
  38.6 0.7 fusion.301
  54.1 0.7 fusion.302
  56.8 0.2 fusion.303
  58.8 0.2 fusion.304
  60.8 0.2 fusion.305
  62.8 0.2 fusion.306
  64.8 0.2 fusion.307
  66.8 0.2 fusion.308
  68.8 0.2 fusion.309
  70.8 0.2 fusion.310
  71.0 0.9 copy-done.1
  72.0 117.1 %reduce-scatter.4.cloned.1.call-done = f32[256,256]{1,0:T(8,128)} async-done(((f32[1024,256]{1,0:T(8,128)}), f32[256,256]{1,0:T(8,128)}) %reduce-scatter.4.cloned.1.call-update) | async-done | bytes 262160 | tf_op jit(solution)/shard_map/reduce_scatter | solution.py:104
  189.2 0.9 copy-done.7
  190.2 1.6 collective-permute-start.3
  191.8 2.3 collective-permute-start.4
  194.1 7.2 %collective-permute-done.3 = f32[256,256]{1,0:T(8,128)S(1)} collective-permute-done((f32[256,256]{1,0:T(8,128)S(1)}, f32[256,256]{1,0:T(8,128)S(1)}, u32[]{:S(2)}, u32[]{:S(2)}) %collective-permute-start.3) | collective-permute-done | bytes 262176 | tf_op jit(solution)/shard_map/ppermute | solution.py:90
  201.3 4.3 collective-permute-done.4
  205.7 5.7 %collective-permute-done.5 = f32[256,256]{1,0:T(8,128)S(1)} collective-permute-done((f32[256,256]{1,0:T(8,128)S(1)}, f32[256,256]{1,0:T(8,128)S(1)}, u32[]{:S(2)}, u32[]{:S(2)}) %collective-permute-start.5) | collective-permute-done | bytes 262176 | tf_op jit(solution)/shard_map/ppermute | solution.py:90
  211.4 0.2 divide_convert_fusion.1
  211.7 33.0 %while.31 = (s32[]{:T(128)}, f32[8,128,256]{2,1,0:T(8,128)S(1)}, s32[]{:T(128)}, s32[]{:T(128)}, s32[32]{0:T(128)S(1)}, /*index=5*/s32[32]{0:T(128)S(1)}, s32[]{...) while((s32[]{:T(128)}, f32[8,128,256]{2,1,0:T(8,128)S(1)}, ...), condition=%wide.region_9.10_spmd, body=%wide.region_8.9_spmd.sunk | while | flops 67633232 | bytes 4982441 | solution.py:49
  212.4 0.7 fusion.327
  227.9 0.7 fusion.328
  230.6 0.2 fusion.329
  232.6 0.2 fusion.330
  234.6 0.2 fusion.331
  236.6 0.2 fusion.332
  238.6 0.2 fusion.333
  240.6 0.2 fusion.334
  242.6 0.2 fusion.335
  244.5 0.2 fusion.336
  244.7 1.0 copy-done.2
  245.8 121.7 %reduce-scatter.6.cloned.1.call-done = f32[256,256]{1,0:T(8,128)} async-done(((f32[1024,256]{1,0:T(8,128)}), f32[256,256]{1,0:T(8,128)}) %reduce-scatter.6.cloned.1.call-update) | async-done | bytes 262160 | tf_op jit(solution)/shard_map/reduce_scatter | solution.py:104
  367.5 0.9 copy-done.8
  368.5 1.5 collective-permute-start.6
  370.1 2.3 collective-permute-start.7
  372.4 7.2 %collective-permute-done.6 = f32[256,256]{1,0:T(8,128)S(1)} collective-permute-done((f32[256,256]{1,0:T(8,128)S(1)}, f32[256,256]{1,0:T(8,128)S(1)}, u32[]{:S(2)}, u32[]{:S(2)}) %collective-permute-start.6) | collective-permute-done | bytes 262176 | tf_op jit(solution)/shard_map/ppermute | solution.py:90
  379.7 4.3 collective-permute-done.7
  384.0 5.7 %collective-permute-done.8 = f32[256,256]{1,0:T(8,128)S(1)} collective-permute-done((f32[256,256]{1,0:T(8,128)S(1)}, f32[256,256]{1,0:T(8,128)S(1)}, u32[]{:S(2)}, u32[]{:S(2)}) %collective-permute-start.8) | collective-permute-done | bytes 262176 | tf_op jit(solution)/shard_map/ppermute | solution.py:90
  389.7 0.2 divide_convert_fusion
  390.1 33.0 %while.32 = (s32[]{:T(128)}, f32[8,128,256]{2,1,0:T(8,128)S(1)}, s32[]{:T(128)}, s32[]{:T(128)}, s32[32]{0:T(128)S(1)}, /*index=5*/s32[32]{0:T(128)S(1)}, s32[]{...) while((s32[]{:T(128)}, f32[8,128,256]{2,1,0:T(8,128)S(1)}, ...), condition=%wide.region_12.13_spmd, body=%wide.region_11.12_spmd.sunk | while | flops 67633232 | bytes 4982441 | solution.py:49
  390.7 0.7 fusion.353
  406.2 0.7 fusion.354
  408.9 0.2 fusion.355
  412.9 0.2 fusion.357
  414.9 0.2 fusion.358
  416.9 0.2 fusion.359
  418.9 0.2 fusion.360
  420.9 0.2 fusion.361
  422.9 0.2 fusion.362
  423.0 1.0 copy-done
  424.0 121.7 %reduce-scatter.8.cloned.1.call-done = f32[256,256]{1,0:T(8,128)} async-done(((f32[1024,256]{1,0:T(8,128)}), f32[256,256]{1,0:T(8,128)}) %reduce-scatter.8.cloned.1.call-update) | async-done | bytes 262160 | tf_op jit(solution)/shard_map/reduce_scatter | solution.py:104
  545.7 1.8 multiply_add_fusion
  (73 shorter events, 1.7 us)
Async XLA Ops:
  6.5 6.6 %copy-start.5 = (s32[1,1,32]{2,1,0:T(1,128)S(1)}, s32[1,1,32]{2,1,0:T(1,128)}, u32[]{:S(2)}) copy-start(s32[1,1,32]{2,1,0:T(1,128)} %param.14) | copy-start | bytes 388
  6.5 20.7 %copy-start.4 = (s32[1,1,32]{2,1,0:T(1,128)S(1)}, s32[1,1,32]{2,1,0:T(1,128)}, u32[]{:S(2)}) copy-start(s32[1,1,32]{2,1,0:T(1,128)} %param.13) | copy-start | bytes 388
  6.5 182.6 %reduce-scatter.4.cloned.1.call-start = ((), (), s32[]{:S(2)}) async-start(), calls=%async_computation.3 | async-start | bytes 1310720 | tf_op jit(solution)/shard_map/reduce_scatter | solution.py:104
  6.5 21.9 %collective-permute-start = (f32[256,256]{1,0:T(8,128)}, f32[256,256]{1,0:T(8,128)S(1)}, u32[]{:S(2)}, u32[]{:S(2)}) collective-permute-start(f32[256,256]{1,0:T(8,128)} %param.17), channel_id=1, source_target_pairs={{0,1},{1,2},{2,3},{3,0},{4,5},{5,6},{6,7},{7,4},{8,9},{9,10},{10,1... | collective-permute-start | bytes 786440 | tf_op jit(solution)/shard_map/ppermute | solution.py:90
  9.6 21.1 %collective-permute-start.1 = (f32[256,256]{1,0:T(8,128)}, f32[256,256]{1,0:T(8,128)S(1)}, u32[]{:S(2)}, u32[]{:S(2)}) collective-permute-start(f32[256,256]{1,0:T(8,128)} %param.17), channel_id=1, source_target_pairs={{0,3},{1,0},{2,1},{3,2},{4,7},{5,4},{6,5},{7,6},{8,11},{9,8},{10,9... | collective-permute-start | bytes 786440 | tf_op jit(solution)/shard_map/ppermute | solution.py:95
  11.6 15.7 %copy-start.6 = (f32[256,256]{1,0:T(8,128)S(1)}, f32[256,256]{1,0:T(8,128)}, u32[]{:S(2)}) copy-start(f32[256,256]{1,0:T(8,128)} %param.17) | copy-start | bytes 786436
  28.5 8.2 %collective-permute-start.2 = (f32[256,256]{1,0:T(8,128)S(1)}, f32[256,256]{1,0:T(8,128)S(1)}, u32[]{:S(2)}, u32[]{:S(2)}) collective-permute-start(f32[256,256]{1,0:T(8,128)S(1)} %collective-permute-done), channel_id=1, source_target_pairs={{0,1},{1,2},{2,3},{3,0},{4,5},{5,6},{6,7},{7,4},{8,9},{9,10},{10,1... | collective-permute-start | bytes 786440 | tf_op jit(solution)/shard_map/ppermute | solution.py:90
  36.7 1.2 copy-start.3
  70.9 1.0 copy-start.1
  70.9 118.3 %copy-start.9 = (s32[256]{0:T(256)S(1)}, s32[256]{0:T(256)}, u32[]{:S(2)}) copy-start(s32[256]{0:T(256)} %param.16) | copy-start | bytes 3076
  71.0 118.3 %copy-start.10 = (s32[256]{0:T(256)S(1)}, s32[256]{0:T(256)}, u32[]{:S(2)}) copy-start(s32[256]{0:T(256)} %param.15) | copy-start | bytes 3076
  71.9 295.5 %reduce-scatter.6.cloned.1.call-start = ((), (), s32[]{:S(2)}) async-start(), calls=%async_computation.4 | async-start | bytes 1310720 | tf_op jit(solution)/shard_map/reduce_scatter | solution.py:104
  189.1 0.9 copy-start.7
  190.2 11.1 %collective-permute-start.3 = (f32[256,256]{1,0:T(8,128)S(1)}, f32[256,256]{1,0:T(8,128)S(1)}, u32[]{:S(2)}, u32[]{:S(2)}) collective-permute-start(f32[256,256]{1,0:T(8,128)S(1)} %get-tuple-element.236), channel_id=1, source_target_pairs={{0,1},{1,2},{2,3},{3,0},{4,5},{5,6},{6,7},{7,4},{8,9},{9,10},{10,1... | collective-permute-start | bytes 786440 | tf_op jit(solution)/shard_map/ppermute | solution.py:90
  191.8 13.9 %collective-permute-start.4 = (f32[256,256]{1,0:T(8,128)S(1)}, f32[256,256]{1,0:T(8,128)S(1)}, u32[]{:S(2)}, u32[]{:S(2)}) collective-permute-start(f32[256,256]{1,0:T(8,128)S(1)} %get-tuple-element.236), channel_id=1, source_target_pairs={{0,3},{1,0},{2,1},{3,2},{4,7},{5,4},{6,5},{7,6},{8,11},{9,8},{10,9... | collective-permute-start | bytes 786440 | tf_op jit(solution)/shard_map/ppermute | solution.py:95
  201.3 10.1 %collective-permute-start.5 = (f32[256,256]{1,0:T(8,128)S(1)}, f32[256,256]{1,0:T(8,128)S(1)}, u32[]{:S(2)}, u32[]{:S(2)}) collective-permute-start(f32[256,256]{1,0:T(8,128)S(1)} %collective-permute-done.3), channel_id=1, source_target_pairs={{0,1},{1,2},{2,3},{3,0},{4,5},{5,6},{6,7},{7,4},{8,9},{9,10},{10,1... | collective-permute-start | bytes 786440 | tf_op jit(solution)/shard_map/ppermute | solution.py:90
  244.7 1.0 copy-start.2
  245.7 300.0 %reduce-scatter.8.cloned.1.call-start = ((), (), s32[]{:S(2)}) async-start(), calls=%async_computation.5 | async-start | bytes 1310720 | tf_op jit(solution)/shard_map/reduce_scatter | solution.py:104
  367.5 0.9 copy-start.8
  368.5 11.1 %collective-permute-start.6 = (f32[256,256]{1,0:T(8,128)S(1)}, f32[256,256]{1,0:T(8,128)S(1)}, u32[]{:S(2)}, u32[]{:S(2)}) collective-permute-start(f32[256,256]{1,0:T(8,128)S(1)} %get-tuple-element.234), channel_id=1, source_target_pairs={{0,1},{1,2},{2,3},{3,0},{4,5},{5,6},{6,7},{7,4},{8,9},{9,10},{10,1... | collective-permute-start | bytes 786440 | tf_op jit(solution)/shard_map/ppermute | solution.py:90
  370.1 13.9 %collective-permute-start.7 = (f32[256,256]{1,0:T(8,128)S(1)}, f32[256,256]{1,0:T(8,128)S(1)}, u32[]{:S(2)}, u32[]{:S(2)}) collective-permute-start(f32[256,256]{1,0:T(8,128)S(1)} %get-tuple-element.234), channel_id=1, source_target_pairs={{0,3},{1,0},{2,1},{3,2},{4,7},{5,4},{6,5},{7,6},{8,11},{9,8},{10,9... | collective-permute-start | bytes 786440 | tf_op jit(solution)/shard_map/ppermute | solution.py:95
  379.6 10.1 %collective-permute-start.8 = (f32[256,256]{1,0:T(8,128)S(1)}, f32[256,256]{1,0:T(8,128)S(1)}, u32[]{:S(2)}, u32[]{:S(2)}) collective-permute-start(f32[256,256]{1,0:T(8,128)S(1)} %collective-permute-done.6), channel_id=1, source_target_pairs={{0,1},{1,2},{2,3},{3,0},{4,5},{5,6},{6,7},{7,4},{8,9},{9,10},{10,1... | collective-permute-start | bytes 786440 | tf_op jit(solution)/shard_map/ppermute | solution.py:90
  423.0 1.0 copy-start
Sparse Core Ops, SparseCore 0:
  72.1 117.0 reduce-scatter.3
  245.8 121.5 reduce-scatter.5
  424.2 121.5 reduce-scatter.7
